TPU v7x, 128 devices: a whole 4x4x4 slice. The times are simulated.
128 devices in a mesh: gx: 8 (over x, core), gy: 16 (over z, y).
Axes of the slice: x: 4, y: 4, z: 4, core: 2. Of those that a mesh axis runs over, the one named last changes fastest.
Arguments:
- eta: float32 [16, 1048576], P(None, ('gx', 'gy')), may hold values from -6 to 6
- forcing: float32 [16, 1048576], P(None, ('gx', 'gy')), may hold values from -3 to 3
- couplings: float32 [3, 1048576], P(None, ('gx', 'gy')), may hold values from 0.02 to 0.3
- neighbors: int32 [3, 1048576], P(None, ('gx', 'gy')), may hold values from 0 to 8703, as said below
- halo_send: int32 [128, 512], P(('gx', 'gy')), may hold values from 0 to 8191
- cycle_send: int32 [128, 128, 128], P(('gx', 'gy')), may hold values from 0 to 8191
- stencil: int32 [3, 2097152], P(None, ('gx', 'gy')), may hold values from 0 to 16383
- stencil_weights: float32 [3, 2097152], P(None, ('gx', 'gy')), as said below
- m_order: int32 [1024], replicated, may hold values from 0 to 1023, as said below
- lat_weights: float32 [1024], replicated, may hold values from 0.5 to 1.5
- love: float32 [1024], replicated, may hold values from 0.1 to 2
- legendre: bfloat16 [1024, 1024, 1024], P(('gx', 'gy')), as said below
Outputs:
- stepped: float32 [16, 1048576], P(None, ('gx', 'gy'))
- loading: float32 [16, 1048576], P(None, ('gx', 'gy'))
Inputs may be any that keep to these rules, and one draw needn't show every extreme that they name: `neighbors`: positions below 8192 are the partition's own cells, the rest its halo cells. `m_order`: each order appears once. legendre[j, l, :] is zero for l < m_order[j]. `stencil_weights`: the 3 weights of a grid point are positive and sum to one.
All inputs are finite; a program needn't handle non-finite values.
Results may differ from a plain program's by a relative error of at most 0.0044.
Values may be sent and summed in bfloat16 or wider, within the bound.
A program may use at most 128 MiB of HBM per device.

v0:
```python
import math

import jax
import jax.numpy as jnp
from jax import lax
from jax.sharding import PartitionSpec as P


def extended_2(cells, sides, width):
    for axis, dim in sides:
        count = lax.axis_size(axis)
        head = lax.slice_in_dim(cells, 0, width, axis=dim)
        tail = lax.slice_in_dim(cells, cells.shape[dim] - width, cells.shape[dim], axis=dim)
        cells = jnp.concatenate(
            [
                lax.ppermute(tail, axis, [(i, (i + 1) % count) for i in range(count)]),
                cells,
                lax.ppermute(head, axis, [((i + 1) % count, i) for i in range(count)]),
            ],
            axis=dim,
        )
    return cells


def wave_tables(m_order, points_count):
    points = jnp.arange(points_count, dtype=jnp.int32)
    phase = points[:, None] * m_order[None, :] % points_count
    angle = phase.astype(jnp.float32) * (2.0 * math.pi / points_count)
    return (jnp.cos(angle), jnp.sin(angle))


def on_device(
    eta,
    forcing,
    couplings,
    neighbors,
    halo_send,
    cycle_send,
    stencil,
    stencil_weights,
    m_order,
    lat_weights,
    love,
    legendre,
):
    fields, per_part = eta.shape
    terms = neighbors.shape[0]
    rim_width = halo_send.shape[1] // 2
    band_count = cycle_send.shape[1]
    slot_count = cycle_send.shape[2]
    orders_here = legendre.shape[0]
    lat_count = legendre.shape[2]
    size_x = lax.axis_size("gx")
    size_y = lax.axis_size("gy")
    partitions = size_x * size_y
    cycles_here = lat_count // partitions
    point_count = stencil.shape[1]
    lon_count = point_count // cycles_here
    degrees = m_order.shape[0]
    eta_rows = eta.T
    rim_values = jnp.take(eta, halo_send[0], axis=1)
    padded = extended_2(rim_values, ((("gx", "gy"), 1),), rim_width)
    extended = jnp.concatenate(
        [eta_rows, padded[:, :rim_width].T, padded[:, 3 * rim_width :].T], axis=0
    )
    picked_cells = jnp.take(extended, neighbors.reshape(-1), axis=0).reshape(
        terms, per_part, fields
    )
    change = jnp.zeros(eta_rows.shape, jnp.float32)
    for which in range(terms):
        change = change + couplings[which][:, None] * (picked_cells[which] - eta_rows)
    stepped_rows = eta_rows + change + forcing.T
    outgoing = jnp.take(stepped_rows, cycle_send[0].reshape(-1), axis=0).reshape(
        band_count, slot_count, fields
    )
    received = lax.all_to_all(outgoing, ("gx", "gy"), split_axis=0, concat_axis=0, tiled=True)
    incoming_rows = received.reshape(-1, fields)
    picked_slots = jnp.take(incoming_rows, stencil.reshape(-1), axis=0).reshape(
        terms, point_count, fields
    )
    gridded_rows = jnp.zeros((point_count, fields), jnp.float32)
    for which in range(terms):
        gridded_rows = gridded_rows + stencil_weights[which][:, None] * picked_slots[which]
    gridded = gridded_rows.T
    cosines, sines = wave_tables(m_order, lon_count)
    scale = lon_count ** (-0.5)
    flat = gridded.reshape(fields * cycles_here, lon_count)
    cosine_part = (
        jnp.dot(flat, cosines, precision=lax.Precision.HIGHEST, preferred_element_type=jnp.float32)
        * scale
    )
    sine_part = (
        jnp.dot(flat, sines, precision=lax.Precision.HIGHEST, preferred_element_type=jnp.float32)
        * scale
    )
    fourier = jnp.stack([cosine_part, sine_part]).astype(jnp.bfloat16)
    fourier = fourier.reshape(2, fields, cycles_here, partitions, orders_here)
    fourier = jnp.transpose(fourier, (3, 4, 0, 1, 2)).reshape(partitions, -1)
    arrived = lax.all_to_all(fourier, ("gx", "gy"), split_axis=0, concat_axis=0, tiled=True)
    arrived = arrived.reshape(partitions, orders_here, 2 * fields, cycles_here)
    spectra = jnp.transpose(arrived, (1, 2, 0, 3)).reshape(orders_here, 2 * fields, lat_count)
    weighted = (spectra.astype(jnp.float32) * lat_weights[None, None, :]).astype(jnp.bfloat16)
    coefficients = jnp.einsum(
        "jci,jli->jcl", weighted, legendre, preferred_element_type=jnp.float32
    )
    scaled = (coefficients * love[None, None, :]).astype(jnp.bfloat16)
    synthesized = jnp.einsum(
        "jcl,jli->jci", scaled, legendre, preferred_element_type=jnp.float32
    ).astype(jnp.bfloat16)
    leaving = synthesized.reshape(orders_here, 2 * fields, partitions, cycles_here)
    leaving = jnp.transpose(leaving, (2, 0, 1, 3)).reshape(partitions, -1)
    returned = lax.all_to_all(leaving, ("gx", "gy"), split_axis=0, concat_axis=0, tiled=True)
    returned = returned.reshape(partitions, orders_here, 2, fields, cycles_here)
    spectral = (
        jnp.transpose(returned, (2, 3, 4, 0, 1))
        .reshape(2, fields * cycles_here, degrees)
        .astype(jnp.float32)
    )
    contract = (((1,), (1,)), ((), ()))
    returned_grid = lax.dot_general(
        spectral[0],
        cosines,
        contract,
        precision=lax.Precision.HIGHEST,
        preferred_element_type=jnp.float32,
    )
    returned_grid = returned_grid + lax.dot_general(
        spectral[1],
        sines,
        contract,
        precision=lax.Precision.HIGHEST,
        preferred_element_type=jnp.float32,
    )
    grid_rows = (returned_grid * scale).reshape(fields, -1).T
    weighted_rows = (stencil_weights[:, :, None] * grid_rows[None, :, :]).reshape(-1, fields)
    slot_rows = (
        jnp.zeros((band_count * slot_count, fields), jnp.float32)
        .at[stencil.reshape(-1)]
        .add(weighted_rows)
    )
    slot_rows = slot_rows.reshape(band_count, slot_count, fields)
    came_back = lax.all_to_all(slot_rows, ("gx", "gy"), split_axis=0, concat_axis=0, tiled=True)
    homeward = came_back.reshape(-1, fields)
    loading_rows = (
        jnp.zeros((per_part, fields), jnp.float32).at[cycle_send[0].reshape(-1)].add(homeward)
    )
    return (stepped_rows.T, loading_rows.T)


def solution(mesh):
    placed = (
        P(None, ("gx", "gy")),
        P(None, ("gx", "gy")),
        P(None, ("gx", "gy")),
        P(None, ("gx", "gy")),
        P(("gx", "gy"), None),
        P(("gx", "gy"), None, None),
        P(None, ("gx", "gy")),
        P(None, ("gx", "gy")),
        P(),
        P(),
        P(),
        P(("gx", "gy"), None, None),
    )
    return jax.shard_map(
        on_device,
        mesh=mesh,
        in_specs=placed,
        out_specs=(P(None, ("gx", "gy")), P(None, ("gx", "gy"))),
        check_vma=False,
    )
```

profile of v0, /device:TPU:1, one launch (start us, length us, event | category | flops | bytes accessed | tf_op | source)
XLA Modules:
  0.0 1084.7 jit_solution(12555045367914837709)
XLA Ops:
  11.2 5.6 collective-permute-start.1
  26.9 83.7 %gather_fusion.1 = f32[24576,16]{1,0:T(8,128)} fusion(f32[8704,16]{1,0:T(8,128)} %copy.112, s32[24576]{0:T(1024)S(1)} %broadcast_clamp_fusion.1), kind=kCustom, calls=%fused_computation.1 | custom fusion | bytes 3244032 | tf_op jit(solution)/shard_map/jit(_take)/gather | solution.py:66
  110.7 7.6 copy.113
  121.4 56.7 %gather_fusion.2 = f32[16384,16]{1,0:T(8,128)} fusion(f32[8192,16]{1,0:T(8,128)} %copy.114, s32[16384]{0:T(1024)S(1)} %broadcast_clamp_fusion.2), kind=kCustom, calls=%fused_computation.2 | custom fusion | bytes 2162688 | tf_op jit(solution)/shard_map/jit(_take)/gather | solution.py:73
  178.0 5.1 copy.115
  184.3 6.2 all-to-all-start
  190.5 18.6 %all-to-all-done = f32[128,128,16]{1,2,0:T(8,128)S(1)} async-done(((f32[128,128,16]{1,2,0:T(8,128)}), f32[128,128,16]{1,2,0:T(8,128)S(1)}, u32[]{:S(2)}, u32[]{:S(2)}) %all-to-all-start) | async-done | bytes 1048608 | tf_op jit(solution)/shard_map/all_to_all | solution.py:76
  209.1 4.6 copy.116
  213.7 165.6 %gather_fusion.3 = f32[49152,16]{1,0:T(8,128)} fusion(f32[16384,16]{1,0:T(8,128)} %bitcast.72, s32[49152]{0:T(1024)S(1)} %broadcast_clamp_fusion), kind=kCustom, calls=%fused_computation.3 | custom fusion | bytes 6488064 | tf_op jit(solution)/shard_map/jit(_take)/gather | solution.py:78
  379.3 26.4 %broadcast_select_fusion = f32[49152,16]{1,0:T(8,128)S(1)} fusion(f32[49152,16]{1,0:T(8,128)} %gather_fusion.3, pred[49152]{0:T(1024)(128)(4,1)S(1)} %compare_and_fusion), kind=kLoop, calls=%fused_computation.9 | loop fusion | flops 786432 | bytes 6340608 | tf_op jit(solution)/shard_map/jit(_take)/select_n | solution.py:78
  405.6 8.7 fusion.4
  414.4 5.1 copy.117
  419.7 35.3 %fusion.39 = bf16[128,1024]{1,0:T(8,128)(2,1)S(1)} fusion(f32[128,2048]{1,0:T(8,128)S(1)} %reshape.241, s32[1024]{0:T(1024)S(1)} %copy-done.10), kind=kOutput, calls=%fused_computation.42 | convolution fusion | flops 3250847744 | bytes 1314816 | tf_op jit(solution)/shard_map/dot_general | solution.py:93
  455.0 35.5 %fusion.36 = bf16[128,1024]{1,0:T(8,128)(2,1)S(1)} fusion(f32[128,2048]{1,0:T(8,128)S(1)} %reshape.241, s32[1024]{0:T(1024)S(1)} %copy-done.10), kind=kOutput, calls=%fused_computation.41 | convolution fusion | flops 3250847744 | bytes 1314816 | tf_op jit(solution)/shard_map/dot_general | solution.py:89
  490.5 5.9 stack.10
  496.4 6.0 stack.9
  502.4 8.6 maximum_bitcast_fusion
  511.0 6.9 copy.118
  520.1 18.3 %all_to_all.28 = bf16[128,2,1024]{2,1,0:T(2,128)(2,1)S(1)} all-to-all(bf16[128,2,1024]{2,1,0:T(2,128)(2,1)S(1)} %reshape.301), channel_id=1, replica_groups=mesh['gx'=8,'gy'=16] {'gx','gy'}, dimensions={0} | all-to-all | bytes 1048576 | tf_op jit(solution)/shard_map/all_to_all | solution.py:99
  545.2 14.6 %convolution_convert_fusion = bf16[8,32,1024]{2,1,0:T(8,128)(2,1)S(1)} fusion(bf16[8,1024,1024]{2,1,0:T(8,128)(2,1)} %param.23, f32[8,32,1024]{2,1,0:T(8,128)S(1)} %copy.122, f32[1024]{0:T(1024)S(1)} %copy-done.8, f32[1024]{0:T(1024)S(1)} %copy-done.9), kind=kOutput, calls=%fused_computation.37 | convolution fusion | flops 1075052544 | bytes 18358272 | tf_op jit(solution)/shard_map/jcl,jli->jci/dot_general | solution.py:107
  564.6 4.3 all-to-all-start.2
  569.1 13.9 %all-to-all-done.2 = bf16[128,2,1024]{2,1,0:T(2,128)(2,1)S(1)} async-done(((bf16[128,2,1024]{2,1,0:T(2,128)(2,1)}), bf16[128,2,1024]{2,1,0:T(2,128)(2,1)S(1)}, u32[]{:S(2)}, u32[]{:S(2)}) %all-to-all-start.2) | async-done | bytes 524320 | tf_op jit(solution)/shard_map/all_to_all | solution.py:112
  587.6 7.0 squeeze.19
  594.6 36.4 %fusion.11 = f32[128,2048]{1,0:T(8,128)} fusion(bf16[128,1024]{1,0:T(8,128)(2,1)S(1)} %squeeze.19, s32[1024]{0:T(1024)S(1)} %copy-done.10), kind=kOutput, calls=%fused_computation.25 | convolution fusion | flops 3250585600 | bytes 1314816 | tf_op jit(solution)/shard_map/dot_general | solution.py:120
  634.2 7.0 squeeze.20
  641.2 37.2 %fusion.24 = f32[128,2048]{1,0:T(8,128)S(1)} fusion(f32[128,2048]{1,0:T(8,128)} %fusion.11, bf16[128,1024]{1,0:T(8,128)(2,1)S(1)} %squeeze.20, s32[1024]{0:T(1024)S(1)} %copy-done.10), kind=kOutput, calls=%fused_computation.32 | convolution fusion | flops 3251109888 | bytes 2363392 | tf_op jit(solution)/shard_map/dot_general | solution.py:127
  681.9 12.3 %copy.129 = f32[49152,16]{1,0:T(8,128)} copy(f32[49152,16]{0,1:T(8,128)S(1)} %broadcast_multiply_fusion) | data formatting | bytes 6291456 | tf_op jit(solution)/shard_map/mul | solution.py:135
  694.2 264.5 %scatter_custom_fusion = f32[16384,16]{1,0:T(8,128)} fusion(s32[49152]{0:T(1024)} %bitcast.91, f32[49152,16]{1,0:T(8,128)} %copy.129, f32[]{:T(128)} %constant.75.clone.1), kind=kCustom, calls=%fused_computation.29 | custom fusion | flops 786432 | bytes 1049088 | tf_op jit(solution)/shard_map/scatter-add | solution.py:139
  958.6 5.1 copy.130
  963.7 22.6 %all_to_all.29 = f32[128,128,16]{1,2,0:T(8,128)S(1)} all-to-all(f32[128,128,16]{1,2,0:T(8,128)S(1)} %copy.130), channel_id=1, replica_groups=mesh['gx'=8,'gy'=16] {'gx','gy'}, dimensions={0} | all-to-all | bytes 2097152 | tf_op jit(solution)/shard_map/all_to_all | solution.py:142
  986.4 4.6 copy.134
  991.0 89.8 %scatter_custom_fusion.1 = f32[8192,16]{1,0:T(8,128)} fusion(s32[16384]{0:T(1024)} %bitcast.100, f32[16384,16]{1,0:T(8,128)} %bitcast.80, f32[]{:T(128)} %constant.75.clone.1), kind=kCustom, calls=%fused_computation.33 | custom fusion | flops 262144 | bytes 524800 | tf_op jit(solution)/shard_map/scatter-add | solution.py:145
  (80 shorter events, 53.4 us)
Async XLA Ops:
  0.6 23.5 %copy-start = (f32[16,8192]{1,0:T(8,128)S(1)}, f32[16,8192]{1,0:T(8,128)}, u32[]{:S(2)}) copy-start(f32[16,8192]{1,0:T(8,128)} %param.12) | copy-start | bytes 1572868
  0.6 23.3 %copy-start.6 = (s32[1,128,128]{2,1,0:T(8,128)S(1)}, s32[1,128,128]{2,1,0:T(8,128)}, u32[]{:S(2)}) copy-start(s32[1,128,128]{2,1,0:T(8,128)} %param.17) | copy-start | bytes 196612
  0.7 23.3 %copy-start.2 = (s32[3,16384]{1,0:T(4,128)S(1)}, s32[3,16384]{1,0:T(4,128)}, u32[]{:S(2)}) copy-start(s32[3,16384]{1,0:T(4,128)} %param.18) | copy-start | bytes 589828
  9.0 15.1 %collective-permute-start = (f32[16,256]{1,0:T(8,128)S(1)}, f32[16,256]{1,0:T(8,128)S(1)}, u32[]{:S(2)}, u32[]{:S(2)}) collective-permute-start(f32[16,256]{1,0:T(8,128)S(1)} %get-tuple-element.22), channel_id=1, source_target_pairs={{0,1},{1,2},{2,3},{3,4},{4,5},{5,6},{6,7},{7,8},{8,9},{9,10},{10,1... | collective-permute-start | bytes 49160 | tf_op jit(solution)/shard_map/ppermute | solution.py:16
  11.2 12.9 %collective-permute-start.1 = (f32[16,256]{1,0:T(8,128)S(1)}, f32[16,256]{1,0:T(8,128)S(1)}, u32[]{:S(2)}, u32[]{:S(2)}) collective-permute-start(f32[16,256]{1,0:T(8,128)S(1)} %get-tuple-element.23), channel_id=1, source_target_pairs={{1,0},{2,1},{3,2},{4,3},{5,4},{6,5},{7,6},{8,7},{9,8},{10,9},{11,1... | collective-permute-start | bytes 49160 | tf_op jit(solution)/shard_map/ppermute | solution.py:18
  21.0 1.4 copy-start.7
  22.4 1.7 copy-start.4
  110.7 7.7 copy-start.5
  118.6 59.4 %copy-start.1 = (f32[8192,16]{0,1:T(8,128)}, f32[8192,16]{0,1:T(8,128)S(1)}, u32[]{:S(2)}) copy-start(f32[8192,16]{0,1:T(8,128)S(1)} %fusion.45) | copy-start | bytes 1572868
  184.3 24.9 %all-to-all-start = ((f32[128,128,16]{1,2,0:T(8,128)}), f32[128,128,16]{1,2,0:T(8,128)S(1)}, u32[]{:S(2)}, u32[]{:S(2)}) async-start(f32[128,128,16]{1,2,0:T(8,128)} %broadcast_select_fusion.2), calls=%async_computation | async-start | bytes 2097152 | tf_op jit(solution)/shard_map/all_to_all | solution.py:76
  414.4 5.3 copy-start.10
  520.0 25.1 %copy-start.8 = (f32[1024]{0:T(1024)S(1)}, f32[1024]{0:T(1024)}, u32[]{:S(2)}) copy-start(f32[1024]{0:T(1024)} %param.22) | copy-start | bytes 12292
  520.1 25.1 %copy-start.9 = (f32[1024]{0:T(1024)S(1)}, f32[1024]{0:T(1024)}, u32[]{:S(2)}) copy-start(f32[1024]{0:T(1024)} %param.21) | copy-start | bytes 12292
  559.9 9.1 copy-start.3
  564.6 18.4 %all-to-all-start.2 = ((bf16[128,2,1024]{2,1,0:T(2,128)(2,1)}), bf16[128,2,1024]{2,1,0:T(2,128)(2,1)S(1)}, u32[]{:S(2)}, u32[]{:S(2)}) async-start(bf16[128,2,1024]{2,1,0:T(2,128)(2,1)} %reshape.303), calls=%async_computation.2 | async-start | bytes 1048576 | tf_op jit(solution)/shard_map/all_to_all | solution.py:112
where the time goes:
time: 1090 us; the launch traced here: 1080 us
  local copies, waits for them, and re-layouts  428 us (39%)
  other arithmetic  405 us (37%)
  matrix products  159 us (15%)
  blocking collectives  40.9 us (4%)
  waiting for transfers between devices  32.6 us (3%)
  starting transfers between devices  18.3 us (2%)
    scatter-add x1, other arithmetic, on_device(): slot_rows = jnp.zeros((band_count * slot_count, fields), jnp.float32).at[...  264 us
    gather x1, local copies, waits for them, and re-layouts, on_device(): jnp.take(incoming_rows, stencil.reshape(-1), axis=0)  166 us
    gather x2, local copies, waits for them, and re-layouts, on_device(): jnp.take(extended, neighbors.reshape(-1), axis=0)  91.3 us
    scatter-add x1, other arithmetic, on_device(): jnp.zeros((per_part, fields), jnp.float32).at[cycle_send[0].reshape(-1)]  89.8 us
    gather x2, local copies, waits for them, and re-layouts, on_device(): jnp.take(stepped_rows, cycle_send[0].reshape(-1), axis=0)  61.8 us
    dot_general x1, matrix products, on_device(): lax.dot_general(spectral[1], sines, contract, precision=lax.Precision.HIG...  37.2 us
    dot_general x1, matrix products, on_device(): lax.dot_general(spectral[0], cosines, contract, precision=lax.Precision.H...  36.4 us
    dot_general x1, matrix products, on_device(): jnp.dot(flat, cosines, precision=lax.Precision.HIGHEST, preferred_element...  35.5 us
  transfers between devices with their start and end apart: 4, of which 2 were waited for; matrix products, arithmetic and copies ran while one was open for 1% of the time, Pallas kernels for 0%

commit v1 on v0

v1 whole, which is shorter than its diff:
```python
import functools
import math

import jax
import jax.numpy as jnp
import numpy as np
from jax import lax
from jax.experimental import pallas as pl
from jax.experimental.pallas import tpu as pltpu
from jax.sharding import PartitionSpec as P

BF = jnp.bfloat16
F32 = jnp.float32
I32 = jnp.int32
F = 16
W = 256
NT = (((1,), (1,)), ((), ()))


def lane_one_hot(row):
    n = row.shape[1]
    return jnp.where(lax.broadcasted_iota(I32, (W, n), 0) == (row & (W - 1)), 1.0, 0.0).astype(BF)


def gather(table, row):
    n = row.shape[1]
    picked = jnp.dot(table, lane_one_hot(row), preferred_element_type=F32)
    group = jnp.broadcast_to(row >> 8, (F, n))
    out = picked[:F]
    for g in range(1, table.shape[0] // F):
        out = jnp.where(group == g, picked[g * F : (g + 1) * F], out)
    return out


def spread(values, row, groups):
    n = row.shape[1]
    group = jnp.broadcast_to((row >> 8).astype(F32), (F, n)).astype(BF)
    return jnp.concatenate(
        [jnp.where(group == BF(g), values, BF(0)) for g in range(groups)], axis=0
    )


def aligned(start, step):
    return pl.multiple_of(start, step)


def index_row(ref, block, rows):
    part = ref[0, pl.ds(aligned(block * rows, rows), rows), :]
    return jnp.concatenate([part[r : r + 1] for r in range(rows)], axis=1)


def halo_kernel(eta_ref, send_ref, low_ref, high_ref):
    table = jnp.concatenate(
        [eta_ref[:, g * W : (g + 1) * W].astype(BF) for g in range(32)], axis=0
    )
    rim = gather(table, send_ref[...]).astype(BF)
    low_ref[...] = rim[:, :W]
    high_ref[...] = rim[:, W:]


def step_kernel(
    eta_ref, forcing_ref, coup_ref, nbr_ref, below_ref, above_ref, send_ref,
    stepped_ref, out_ref, table, table2,
):
    for g in range(32):
        table[g * F : (g + 1) * F] = eta_ref[:, g * W : (g + 1) * W].astype(BF)
    table[32 * F : 33 * F] = below_ref[...]
    table[33 * F : 34 * F] = above_ref[...]

    def step(b, carry):
        at = pl.ds(aligned(b * 512, 512), 512)
        here = eta_ref[:, at]
        total = here + forcing_ref[:, at]
        for k in range(3):
            total += coup_ref[k : k + 1, at] * (gather(table[...], nbr_ref[k : k + 1, at]) - here)
        stepped_ref[:, at] = total
        rounded = total.astype(BF)
        table2[pl.ds(aligned(b * 32, 32), F)] = rounded[:, :W]
        table2[pl.ds(aligned(b * 32 + F, F), F)] = rounded[:, W:]
        return carry

    lax.fori_loop(0, 16, step, 0)

    def send(b, carry):
        row = index_row(send_ref, b, 8)
        for half in range(2):
            got = gather(table2[...], row[:, half * 512 : half * 512 + 512]).astype(BF)
            for r in range(4):
                out_ref[b * 8 + half * 4 + r] = got[:, r * 128 : r * 128 + 128]
        return carry

    lax.fori_loop(0, 16, send, 0)


def order_slot(row):
    return (row & 1) * 512 + (row >> 1)


def grid_kernel(
    in_ref, sten_ref, wts_ref, m_ref, wave_hbm, wave_lo_hbm, out_ref,
    table, grid, wave, wave_lo, sems,
):
    copies = [
        pltpu.make_async_copy(wave_hbm, wave, sems.at[0]),
        pltpu.make_async_copy(wave_lo_hbm, wave_lo, sems.at[1]),
    ]
    for c in copies:
        c.start()
    for g in range(64):
        table[g * F : (g + 1) * F, :128] = in_ref[2 * g]
        table[g * F : (g + 1) * F, 128:] = in_ref[2 * g + 1]

    def pick(b, carry):
        at = pl.ds(aligned(b * 512, 512), 512)
        total = jnp.zeros((F, 512), F32)
        for k in range(3):
            total += gather(table[...], sten_ref[k : k + 1, at]) * wts_ref[k : k + 1, at]
        grid[pl.ds(aligned(b // 4 * F, F), F), pl.ds(aligned(b % 4 * 512, 512), 512)] = total
        return carry

    lax.fori_loop(0, 32, pick, 0)
    for c in copies:
        c.wait()
    scale = 2048.0**-0.5
    parts = []
    for parity in range(2):
        near, far = grid[:, :1024], grid[:, 1024:]
        folded = near + far if parity == 0 else near - far
        high = folded.astype(BF)
        low = (folded - high.astype(F32)).astype(BF)
        both = jnp.concatenate([high, low], axis=0)
        first = lax.dot_general(wave[parity], both, NT, preferred_element_type=F32)
        second = lax.dot_general(wave_lo[parity], high, NT, preferred_element_type=F32)
        parts.append(((first[:, :128] + first[:, 128:] + second) * scale).astype(BF))
    slot = jnp.broadcast_to(order_slot(m_ref[...]).astype(F32), (128, 1024))
    column = jnp.concatenate(
        [slot[:, r * 128 : r * 128 + 128].T for r in range(8)], axis=0
    ).astype(I32)
    lane = lax.broadcasted_iota(I32, (1024, 128), 1)
    chosen = jnp.concatenate(
        [jnp.where(column == lane + r * 128, 1.0, 0.0).astype(BF) for r in range(8)], axis=1
    )
    rows = []
    for c in range(2):
        source = jnp.concatenate([parts[0][c * 512 : c * 512 + 512], parts[1][c * 512 : c * 512 + 512]], axis=0)
        rows.append(jnp.dot(chosen, source, preferred_element_type=F32).reshape(128, 8, 128))
    out_ref[...] = jnp.concatenate(rows, axis=1).astype(BF)


def order_kernel(in_ref, lat_ref, love_ref, leg_ref, out_ref, wide, left, right):
    j = pl.program_id(0)

    def shuffle(flip):
        a = lax.broadcasted_iota(I32, (1024, 1024), 1 if flip else 0)
        b = lax.broadcasted_iota(I32, (1024, 1024), 0 if flip else 1)
        return jnp.where((b >> 3) + (b & 7) * 128 == a, 1.0, 0.0).astype(BF)

    @pl.when(j == 0)
    def _():
        wide[...] = in_ref[...].astype(F32).reshape(2048, 128)
        blocks = []
        for o in range(8):
            for c in range(2):
                turned = wide[pl.ds(c * 8 + o, 128, stride=16), :].T
                blocks.append(
                    jnp.concatenate([turned[i * F : (i + 1) * F] for i in range(8)], axis=1)
                )
        spectra = jnp.dot(
            jnp.concatenate(blocks, axis=0).astype(BF), shuffle(False), preferred_element_type=F32
        )
        left[...] = (spectra * lat_ref[...]).astype(BF)

    at = pl.ds(aligned(j * 32, 32), 32)
    legendre = leg_ref[0]
    coefficients = lax.dot_general(left[at], legendre, NT, preferred_element_type=F32)
    scaled = (coefficients * love_ref[...]).astype(BF)
    right[at] = jnp.dot(scaled, legendre, preferred_element_type=F32).astype(BF)

    @pl.when(j == 7)
    def _():
        back = jnp.dot(right[...], shuffle(True), preferred_element_type=F32)
        for o in range(8):
            for c in range(2):
                block = back[(o * 2 + c) * F : (o * 2 + c + 1) * F]
                turned = jnp.concatenate(
                    [block[:, i * 128 : i * 128 + 128] for i in range(8)], axis=0
                ).T
                wide[pl.ds(c * 8 + o, 128, stride=16), :] = turned
        out_ref[...] = wide[...].reshape(128, 16, 128).astype(BF)


def slot_kernel(
    in_ref, sten_ref, wts_ref, m_ref, wave_hbm, wave_lo_hbm, out_ref,
    grid, sums, wave, wave_lo, sems,
):
    copies = [
        pltpu.make_async_copy(wave_hbm, wave, sems.at[0]),
        pltpu.make_async_copy(wave_lo_hbm, wave_lo, sems.at[1]),
    ]
    for c in copies:
        c.start()
    arrived = in_ref[...].astype(F32)
    slot = order_slot(m_ref[...])
    chosen = jnp.where(lax.broadcasted_iota(I32, (1024, 1024), 0) == slot, 1.0, 0.0).astype(BF)
    turned = []
    for c in range(2):
        rows = arrived[:, c * 8 : c * 8 + 8].reshape(1024, 128).astype(BF)
        placed = jnp.dot(chosen, rows, preferred_element_type=F32)
        turned.append(
            jnp.concatenate([placed[r * 128 : r * 128 + 128].T for r in range(8)], axis=1).astype(BF)
        )
    for c in copies:
        c.wait()
    sides = []
    for parity in range(2):
        at = slice(parity * 512, parity * 512 + 512)
        source = jnp.concatenate([turned[0][:, at], turned[1][:, at]], axis=1)
        sides.append(
            jnp.dot(source, wave[parity], preferred_element_type=F32)
            + jnp.dot(source, wave_lo[parity], preferred_element_type=F32)
        )
    scale = 2048.0**-0.5
    grid[:, :1024] = (sides[0] + sides[1]) * scale
    grid[:, 1024:] = (sides[0] - sides[1]) * scale
    sums[...] = jnp.zeros_like(sums)

    def add(b, carry):
        at = pl.ds(aligned(b * 1024, 1024), 1024)
        here = grid[pl.ds(aligned(b // 2 * F, F), F), pl.ds(aligned(b % 2 * 1024, 1024), 1024)]
        left, right = [], []
        for k in range(3):
            row = sten_ref[k : k + 1, at]
            left.append(spread((here * wts_ref[k : k + 1, at]).astype(BF), row, 64))
            right.append(lane_one_hot(row))
        sums[...] += lax.dot_general(
            jnp.concatenate(left, axis=1), jnp.concatenate(right, axis=1), NT,
            preferred_element_type=F32,
        )
        return carry

    lax.fori_loop(0, 16, add, 0)
    for g in range(64):
        out_ref[2 * g] = sums[g * F : (g + 1) * F, :128].astype(BF)
        out_ref[2 * g + 1] = sums[g * F : (g + 1) * F, 128:].astype(BF)


def home_kernel(in_ref, send_ref, out_ref, sums):
    sums[...] = jnp.zeros_like(sums)

    def add(b, carry):
        row = index_row(send_ref, b, 8)
        values = jnp.concatenate([in_ref[b * 8 + r] for r in range(8)], axis=1)
        sums[...] += lax.dot_general(
            spread(values, row, 32), lane_one_hot(row), NT, preferred_element_type=F32
        )
        return carry

    lax.fori_loop(0, 16, add, 0)
    for g in range(32):
        out_ref[:, g * W : (g + 1) * W] = sums[g * F : (g + 1) * F]


VM = pl.BlockSpec(memory_space=pltpu.VMEM)
ANY = pl.BlockSpec(memory_space=pl.ANY)


def call(kernel, out_shape, in_specs, scratch, *args):
    return pl.pallas_call(
        kernel,
        out_shape=out_shape,
        in_specs=in_specs,
        out_specs=jax.tree.map(lambda _: VM, out_shape),
        scratch_shapes=scratch,
        compiler_params=pltpu.CompilerParams(vmem_limit_bytes=56 << 20),
    )(*args)


def shape(dims, kind=BF):
    return jax.ShapeDtypeStruct(dims, kind)


def waves():
    m = np.arange(1024)
    n = np.arange(1024)
    angle = 2.0 * math.pi * ((m[:, None] * n[None, :]) % 2048) / 2048.0
    table = np.stack([np.cos(angle), np.sin(angle)])
    table = np.stack([table[:, p::2].reshape(1024, 1024) for p in range(2)])
    high = table.astype(BF)
    return high, (table - high.astype(np.float64)).astype(BF)


AXES = ("gx", "gy")
PACK = (128, F, 128)


def exchange(blocks):
    return lax.all_to_all(blocks, AXES, split_axis=0, concat_axis=0, tiled=True)


def on_device(
    eta, forcing, couplings, neighbors, halo_send, cycle_send, stencil, stencil_weights,
    m_order, lat_weights, love, legendre,
):
    parts = lax.axis_size("gx") * lax.axis_size("gy")
    m_row = m_order.reshape(1, -1)
    wave, wave_lo = (jnp.asarray(t) for t in waves())
    low, high = call(halo_kernel, (shape((F, W)), shape((F, W))), [VM] * 2, [], eta, halo_send)
    below = lax.ppermute(high, AXES, [(i, (i + 1) % parts) for i in range(parts)])
    above = lax.ppermute(low, AXES, [((i + 1) % parts, i) for i in range(parts)])
    stepped, leaving = call(
        step_kernel, (shape(eta.shape, F32), shape(PACK)), [VM] * 7,
        [pltpu.VMEM((34 * F, W), BF), pltpu.VMEM((32 * F, W), BF)],
        eta, forcing, couplings, neighbors, below, above, cycle_send,
    )
    incoming = exchange(leaving)
    wave_scratch = [
        pltpu.VMEM((2, 1024, 1024), BF), pltpu.VMEM((2, 1024, 1024), BF),
        pltpu.SemaphoreType.DMA((2,)),
    ]
    fourier = call(
        grid_kernel, shape(PACK), [VM] * 4 + [ANY] * 2,
        [pltpu.VMEM((64 * F, W), BF), pltpu.VMEM((128, 2048), F32)] + wave_scratch,
        incoming, stencil, stencil_weights, m_row, wave, wave_lo,
    )
    spectra = exchange(fourier)
    whole = lambda *dims: pl.BlockSpec(dims, lambda j: (0,) * len(dims))
    synthesized = pl.pallas_call(
        order_kernel,
        out_shape=shape(PACK),
        grid=(8,),
        in_specs=[
            whole(*PACK), whole(1, 1024), whole(1, 1024),
            pl.BlockSpec((1, 1024, 1024), lambda j: (j, 0, 0)),
        ],
        out_specs=whole(*PACK),
        scratch_shapes=[
            pltpu.VMEM((2048, 128), F32), pltpu.VMEM((256, 1024), BF), pltpu.VMEM((256, 1024), BF),
        ],
        compiler_params=pltpu.CompilerParams(vmem_limit_bytes=56 << 20),
    )(spectra, lat_weights.reshape(1, -1), love.reshape(1, -1), legendre)
    returned = exchange(synthesized)
    slots = call(
        slot_kernel, shape(PACK), [VM] * 4 + [ANY] * 2,
        [pltpu.VMEM((128, 2048), F32), pltpu.VMEM((64 * F, W), F32)] + wave_scratch,
        returned, stencil, stencil_weights, m_row, wave, wave_lo,
    )
    homeward = exchange(slots)
    loading = call(
        home_kernel, shape(eta.shape, F32), [VM] * 2, [pltpu.VMEM((32 * F, W), F32)],
        homeward, cycle_send,
    )
    return stepped, loading


def solution(mesh):
    both = ("gx", "gy")
    cells = P(None, both)
    placed = (
        cells, cells, cells, cells, P(both, None), P(both, None, None), cells, cells,
        P(), P(), P(), P(both, None, None),
    )
    return jax.shard_map(
        on_device, mesh=mesh, in_specs=placed, out_specs=(cells, cells), check_vma=False
    )
```

time: 1090 us -> 213 us (0.20)
  local copies, waits for them, and re-layouts: 428 us -> 1.19 us
  other arithmetic: 405 us -> 0 us
  matrix products: 159 us -> 0 us
  Pallas kernels: 0 us -> 120 us
  blocking collectives: 40.9 us -> 81.2 us
  waiting for transfers between devices: 32.6 us -> 1.54 us
    scatter-add x2 -> x0, other arithmetic: 354 us -> none  [the longest x1 264 us: on_device(): slot_rows = jnp.zeros((band_count * slot_count, fields), jnp.float32).at[...]
    gather x7 -> x0, local copies, waits for them, and re-layouts: 322 us -> none  [the longest x1 166 us: on_device(): jnp.take(incoming_rows, stencil.reshape(-1), axis=0)]
    dot_general x5 -> x0, matrix products: 159 us -> none  [the longest x1 37.2 us: on_device(): lax.dot_general(spectral[1], sines, contract, precision=lax.Precision.HIG...]
    pallas_call x0 -> x6, Pallas kernels: none -> 120 us  [the longest x5 105 us: call(): pl.pallas_call(kernel, out_shape=out_shape, in_specs=in_specs, out_specs=...]
    all_to_all x2 -> x4, blocking collectives: 40.9 us -> 81.2 us  [exchange(): return lax.all_to_all(blocks, AXES, split_axis=0, concat_axis=0, tiled=True)]
    all_to_all x2 -> x0, waiting for transfers between devices: 32.6 us -> none  [the longest x1 18.6 us: on_device(): lax.all_to_all(outgoing, ('gx', 'gy'), split_axis=0, concat_axis=0, tiled...]
    select_n x8 -> x0, other arithmetic: 29.6 us -> none  [the longest x1 26.4 us: on_device(): jnp.take(incoming_rows, stencil.reshape(-1), axis=0)]
    transpose x2 -> x0, other arithmetic: 17.3 us -> none  [the longest x1 8.73 us: on_device(): gridded = gridded_rows.T]
  transfers between devices with their start and end apart: 4 -> 2, of which waited for: 2 -> 1; matrix products, arithmetic and copies ran while one was open for 1% -> 0% of each run, Pallas kernels for 0% -> 0%
where the time goes in v1:
time: 213 us; the launch traced here: 212 us
  Pallas kernels  120 us (56%)
  blocking collectives  81.2 us (38%)
  starting transfers between devices  7.6 us (4%)
    pallas_call x5, Pallas kernels, call(): pl.pallas_call(kernel, out_shape=out_shape, in_specs=in_specs, out_specs=...  105 us
    all_to_all x4, blocking collectives, exchange(): return lax.all_to_all(blocks, AXES, split_axis=0, concat_axis=0, tiled=True)  81.2 us
    pallas_call x1, Pallas kernels, on_device(): pl.pallas_call(order_kernel, out_shape=shape(PACK), grid=(8,), in_specs=[...  15.3 us
    ppermute x1, starting transfers between devices, on_device(): lax.ppermute(low, AXES, [((i + 1) % parts, i) for i in range(parts)])  5.47 us
  transfers between devices with their start and end apart: 2, of which 1 were waited for; matrix products, arithmetic and copies ran while one was open for 0% of the time, Pallas kernels for 0%

profile of v1, /device:TPU:1, one launch (start us, length us, event | category | flops | bytes accessed | tf_op | source)
XLA Modules:
  0.0 212.2 jit_solution(4969221547618697923)
XLA Ops:
  0.6 1.9 shard_map.149
  2.6 2.1 %collective-permute-start = (bf16[16,256]{1,0:T(8,128)(2,1)}, bf16[16,256]{1,0:T(8,128)(2,1)S(1)}, u32[]{:S(2)}, u32[]{:S(2)}) collective-permute-start(bf16[16,256]{1,0:T(8,128)(2,1)} %get-tuple-element.6), channel_id=1, source_target_pairs={{0,1},{1,2},{2,3},{3,4},{4,5},{5,6},{6,7},{7,8},{8,9},{9,10},{10,1... | collective-permute-start | bytes 24584 | tf_op jit(solution)/shard_map/ppermute | solution.py:308
  4.7 5.5 %collective-permute-start.1 = (bf16[16,256]{1,0:T(8,128)(2,1)}, bf16[16,256]{1,0:T(8,128)(2,1)S(1)}, u32[]{:S(2)}, u32[]{:S(2)}) collective-permute-start(bf16[16,256]{1,0:T(8,128)(2,1)} %get-tuple-element.7), channel_id=1, source_target_pairs={{1,0},{2,1},{3,2},{4,3},{5,4},{6,5},{7,6},{8,7},{9,8},{10,9},{11,1... | collective-permute-start | bytes 24584 | tf_op jit(solution)/shard_map/ppermute | solution.py:309
  10.2 1.5 collective-permute-done.below_ref
  11.7 0.0 copy-start
  11.7 0.0 collective-permute-done.1.above_ref
  11.7 0.6 copy-done
  12.3 0.0 copy-start.1
  12.3 0.6 copy-done.1
  12.9 19.3 %shard_map.150 = (f32[16,8192]{1,0:T(8,128)}, bf16[128,16,128]{2,1,0:T(8,128)(2,1)}) custom-call(f32[16,8192]{1,0:T(8,128)} %eta_ref.3, f32[16,8192]{1,0:T(8,128)} %forcing_ref.1, f32[3,8192]{1,0:T(4,128)} %coup_ref.1, s32[3,8192]{1,0:T(4,128)} %nbr_ref.1, bf16[16,256]{1,0:T(8,128)(2,1)} %copy-done, bf16[16,256]{1,0:T(8,128)(2,1)} %copy-done.1, ...), custom_call_target="tpu_custom_call" | custom-call | tf_op jit(solution)/shard_map/pallas_call | solution.py:268
  32.2 23.7 %all_to_all.20.in_ref = bf16[128,16,128]{2,1,0:T(8,128)(2,1)} all-to-all(bf16[128,16,128]{2,1,0:T(8,128)(2,1)} %get-tuple-element.9), channel_id=1, replica_groups=mesh['gx'=8,'gy'=16] {'gx','gy'}, dimensions={0} | all-to-all | bytes 1048576 | tf_op jit(solution)/shard_map/all_to_all | solution.py:297
  55.9 37.6 %shard_map.151 = bf16[128,16,128]{2,1,0:T(8,128)(2,1)} custom-call(bf16[128,16,128]{2,1,0:T(8,128)(2,1)} %all_to_all.20.in_ref, s32[3,16384]{1,0:T(4,128)} %sten_ref.3, f32[3,16384]{1,0:T(4,128)} %wts_ref.3, s32[1,1024]{1,0:T(1,128)} %bitcast.3, bf16[2,1024,1024]{2,1,0:T(8,128)(2,1)} %constant.4.clone.wave_hbm, bf16[2,1024,1024]{2,1,0:T(8,128)(2,1)} %constant.5.clone.wave_lo_hbm), custom_call_target="tpu_custom_call" | custom-call | tf_op jit(solution)/shard_map/pallas_call | solution.py:268
  93.5 19.2 %all_to_all.21.in_ref = bf16[128,16,128]{2,1,0:T(8,128)(2,1)} all-to-all(bf16[128,16,128]{2,1,0:T(8,128)(2,1)} %shard_map.151), channel_id=1, replica_groups=mesh['gx'=8,'gy'=16] {'gx','gy'}, dimensions={0} | all-to-all | bytes 1048576 | tf_op jit(solution)/shard_map/all_to_all | solution.py:297
  112.6 15.3 %shard_map.152 = bf16[128,16,128]{2,1,0:T(8,128)(2,1)} custom-call(bf16[128,16,128]{2,1,0:T(8,128)(2,1)} %all_to_all.21.in_ref, f32[1,1024]{1,0:T(1,128)} %bitcast.5, f32[1,1024]{1,0:T(1,128)} %bitcast.6, bf16[8,1024,1024]{2,1,0:T(8,128)(2,1)} %leg_ref.1), custom_call_target="tpu_custom_call" | custom-call | tf_op jit(solution)/shard_map/pallas_call | solution.py:327
  128.0 19.2 %all_to_all.22.in_ref = bf16[128,16,128]{2,1,0:T(8,128)(2,1)} all-to-all(bf16[128,16,128]{2,1,0:T(8,128)(2,1)} %shard_map.152), channel_id=1, replica_groups=mesh['gx'=8,'gy'=16] {'gx','gy'}, dimensions={0} | all-to-all | bytes 1048576 | tf_op jit(solution)/shard_map/all_to_all | solution.py:297
  147.1 36.3 %shard_map.153 = bf16[128,16,128]{2,1,0:T(8,128)(2,1)} custom-call(bf16[128,16,128]{2,1,0:T(8,128)(2,1)} %all_to_all.22.in_ref, s32[3,16384]{1,0:T(4,128)} %sten_ref.3, f32[3,16384]{1,0:T(4,128)} %wts_ref.3, s32[1,1024]{1,0:T(1,128)} %bitcast.4, bf16[2,1024,1024]{2,1,0:T(8,128)(2,1)} %constant.4.clone.wave_hbm, bf16[2,1024,1024]{2,1,0:T(8,128)(2,1)} %constant.5.clone.wave_lo_hbm), custom_call_target="tpu_custom_call" | custom-call | tf_op jit(solution)/shard_map/pallas_call | solution.py:268
  183.5 19.2 %all_to_all.23.in_ref = bf16[128,16,128]{2,1,0:T(8,128)(2,1)} all-to-all(bf16[128,16,128]{2,1,0:T(8,128)(2,1)} %shard_map.153), channel_id=1, replica_groups=mesh['gx'=8,'gy'=16] {'gx','gy'}, dimensions={0} | all-to-all | bytes 1048576 | tf_op jit(solution)/shard_map/all_to_all | solution.py:297
  202.6 9.6 %shard_map.154 = f32[16,8192]{1,0:T(8,128)} custom-call(bf16[128,16,128]{2,1,0:T(8,128)(2,1)} %all_to_all.23.in_ref, s32[1,128,128]{2,1,0:T(8,128)} %send_ref.5), custom_call_target="tpu_custom_call" | custom-call | tf_op jit(solution)/shard_map/pallas_call | solution.py:268
Async XLA Ops:
  2.6 9.1 %collective-permute-start = (bf16[16,256]{1,0:T(8,128)(2,1)}, bf16[16,256]{1,0:T(8,128)(2,1)S(1)}, u32[]{:S(2)}, u32[]{:S(2)}) collective-permute-start(bf16[16,256]{1,0:T(8,128)(2,1)} %get-tuple-element.6), channel_id=1, source_target_pairs={{0,1},{1,2},{2,3},{3,4},{4,5},{5,6},{6,7},{7,8},{8,9},{9,10},{10,1... | collective-permute-start | bytes 24584 | tf_op jit(solution)/shard_map/ppermute | solution.py:308
  4.7 7.0 %collective-permute-start.1 = (bf16[16,256]{1,0:T(8,128)(2,1)}, bf16[16,256]{1,0:T(8,128)(2,1)S(1)}, u32[]{:S(2)}, u32[]{:S(2)}) collective-permute-start(bf16[16,256]{1,0:T(8,128)(2,1)} %get-tuple-element.7), channel_id=1, source_target_pairs={{1,0},{2,1},{3,2},{4,3},{5,4},{6,5},{7,6},{8,7},{9,8},{10,9},{11,1... | collective-permute-start | bytes 24584 | tf_op jit(solution)/shard_map/ppermute | solution.py:309
  11.7 0.6 copy-start
  12.3 0.6 copy-start.1

commit v2 on v1

v2 whole, which is shorter than its diff:
```python
import functools
import math

import jax
import jax.numpy as jnp
import numpy as np
from jax import lax
from jax.experimental import pallas as pl
from jax.experimental.pallas import tpu as pltpu
from jax.sharding import PartitionSpec as P

BF = jnp.bfloat16
F32 = jnp.float32
I32 = jnp.int32
F = 16
W = 256
NT = (((1,), (1,)), ((), ()))
MESH = pl.DeviceIdType.MESH
AXES = ("gx", "gy")
PARTS = 128
PACK = (PARTS, F, 128)
SCALE = 2048.0**-0.5


def place(part):
    return (part // 16, lax.rem(part, 16))


def later(part, steps):
    return lax.rem(part + steps, PARTS)


class Exchange:
    def __init__(self, me, out, into, send_sem, recv_sems, group=PARTS):
        self.me, self.out, self.into = me, out, into
        self.send_sem, self.recv_sems, self.group = send_sem, recv_sems, group

    def send(self, steps):
        to = later(self.me, steps)
        pltpu.make_async_remote_copy(
            src_ref=self.out.at[to],
            dst_ref=self.into.at[self.me],
            send_sem=self.send_sem,
            recv_sem=self.recv_sems.at[steps // self.group],
            device_id=place(to),
            device_id_type=MESH,
        ).start()

    def keep(self):
        self.into[self.me] = self.out[self.me]

    def send_all(self):
        def one(steps, carry):
            self.send(steps)
            return carry

        lax.fori_loop(1, PARTS, one, 0)
        self.keep()

    def tiles(self, count, sem):
        at = pl.ds(0, count)
        return pltpu.make_async_remote_copy(
            src_ref=self.out.at[at],
            dst_ref=self.into.at[at],
            send_sem=self.send_sem,
            recv_sem=self.recv_sems.at[sem],
            device_id=place(later(self.me, 1)),
            device_id_type=MESH,
        )

    def wait_group(self, group, count):
        self.tiles(count, group).wait_recv()

    def wait_sent(self):
        self.tiles(PARTS - 1, 0).wait_send()


def lane_one_hot(row):
    n = row.shape[1]
    return jnp.where(lax.broadcasted_iota(I32, (W, n), 0) == (row & (W - 1)), 1.0, 0.0).astype(BF)


def gather(table, row):
    n = row.shape[1]
    picked = jnp.dot(table, lane_one_hot(row), preferred_element_type=F32)
    group = jnp.broadcast_to(row >> 8, (F, n))
    out = picked[:F]
    for g in range(1, table.shape[0] // F):
        out = jnp.where(group == g, picked[g * F : (g + 1) * F], out)
    return out


def spread(values, row, groups):
    n = row.shape[1]
    group = jnp.broadcast_to((row >> 8).astype(F32), (F, n)).astype(BF)
    return jnp.concatenate(
        [jnp.where(group == BF(g), values, BF(0)) for g in range(groups)], axis=0
    )


def aligned(start, step):
    return pl.multiple_of(start, step)


def order_slot(row):
    return (row & 1) * 512 + (row >> 1)


def kernel(
    eta_ref, forcing_ref, coup_ref, nbr_ref, halo_ref, send_ref, sten_hbm, wts_hbm, m_ref, lat_ref,
    love_ref, leg_hbm, wave_hbm, wave_lo_hbm,
    stepped_ref, loading_ref,
    table, table2, rim, slots, grid, wide, left, right, sums, cell_sums, chosen, chosen_t, mix, mix_t,
    sten_ref, wts_ref, leg, wave, wave_lo,
    out0, in0, out1, in1, out2, in2, out3, in3,
    load_sems, leg_sems, halo_send, halo_recv, send_sems, recv0, recv1, recv2, recv3,
):
    me = lax.axis_index("gx") * 16 + lax.axis_index("gy")
    barrier = pltpu.get_barrier_semaphore()

    def greet(steps, carry):
        pl.semaphore_signal(barrier, inc=1, device_id=place(later(me, steps)), device_id_type=MESH)
        return carry

    lax.fori_loop(1, PARTS, greet, 0)
    loads = [
        pltpu.make_async_copy(src, dst, load_sems.at[i])
        for i, (src, dst) in enumerate(
            [(sten_hbm, sten_ref), (wts_hbm, wts_ref), (wave_hbm, wave), (wave_lo_hbm, wave_lo)]
        )
    ]
    leg_loads = [pltpu.make_async_copy(leg_hbm.at[o], leg.at[o], leg_sems.at[o]) for o in range(8)]
    for load in loads + leg_loads:
        load.start()

    for g in range(32):
        table[g * F : (g + 1) * F] = eta_ref[:, g * W : (g + 1) * W].astype(BF)
    rim[...] = gather(table[: 32 * F], halo_ref[...]).astype(BF)
    slot = order_slot(m_ref[...])
    for r in range(8):
        at = slice(r * 128, r * 128 + 128)
        row = lax.broadcasted_iota(I32, (128, 1024), 0) + r * 128
        lane = lax.broadcasted_iota(I32, (128, 1024), 1)
        chosen[at] = jnp.where(slot == row, 1.0, 0.0).astype(BF)
        column = jnp.broadcast_to(slot[:, at].astype(F32), (128, 128)).T.astype(I32)
        for s in range(8):
            side = slice(s * 128, s * 128 + 128)
            chosen_t[at, side] = jnp.where(column == lane[:, side], 1.0, 0.0).astype(BF)
        mix[at] = jnp.where((lane >> 3) + (lane & 7) * 128 == row, 1.0, 0.0).astype(BF)
        mix_t[at] = jnp.where((row >> 3) + (row & 7) * 128 == lane, 1.0, 0.0).astype(BF)

    pl.semaphore_wait(barrier, PARTS - 1)
    halos = []
    for i, (start, to) in enumerate([(W, later(me, 1)), (0, later(me, PARTS - 1))]):
        halos.append(
            pltpu.make_async_remote_copy(
                src_ref=rim.at[:, pl.ds(start, W)],
                dst_ref=table.at[pl.ds((32 + i) * F, F)],
                send_sem=halo_send.at[i],
                recv_sem=halo_recv.at[i],
                device_id=place(to),
                device_id_type=MESH,
            )
        )
    for halo in halos:
        halo.start()
    for halo in halos:
        halo.wait()

    def step(b, carry):
        at = pl.ds(aligned(b * 512, 512), 512)
        here = eta_ref[:, at]
        total = here + forcing_ref[:, at]
        for k in range(3):
            total += coup_ref[k : k + 1, at] * (gather(table[...], nbr_ref[k : k + 1, at]) - here)
        stepped_ref[:, at] = total
        rounded = total.astype(BF)
        table2[pl.ds(aligned(b * 32, 32), F)] = rounded[:, :W]
        table2[pl.ds(aligned(b * 32 + F, F), F)] = rounded[:, W:]
        return carry

    lax.fori_loop(0, 16, step, 0)

    cells = Exchange(me, out0, in0, send_sems.at[0], recv0)

    def send(b, carry):
        for half in range(2):
            steps = [b * 8 + half * 4 + r for r in range(4)]
            row = jnp.concatenate([send_ref[0, pl.ds(later(me, s), 1), :] for s in steps], axis=1)
            got = gather(table2[...], row).astype(BF)
            for r in range(4):
                out0[later(me, steps[r])] = got[:, r * 128 : r * 128 + 128]
                if half + r == 0:
                    pl.when(b > 0)(functools.partial(cells.send, steps[r]))
                else:
                    cells.send(steps[r])
        return carry

    lax.fori_loop(0, 16, send, 0)
    cells.keep()
    for load in loads:
        load.wait()
    cells.wait_group(0, PARTS - 1)
    for g in range(64):
        slots[g * F : (g + 1) * F, :128] = in0[2 * g]
        slots[g * F : (g + 1) * F, 128:] = in0[2 * g + 1]

    def pick(b, carry):
        at = pl.ds(aligned(b * 512, 512), 512)
        total = jnp.zeros((F, 512), F32)
        for k in range(3):
            total += gather(slots[...], sten_ref[k : k + 1, at]) * wts_ref[k : k + 1, at]
        grid[pl.ds(aligned(b // 4 * F, F), F), pl.ds(aligned(b % 4 * 512, 512), 512)] = total
        return carry

    lax.fori_loop(0, 32, pick, 0)

    halves = []
    for parity in range(2):
        near, far = grid[:, :1024], grid[:, 1024:]
        folded = near + far if parity == 0 else near - far
        high = folded.astype(BF)
        low = (folded - high.astype(F32)).astype(BF)
        both = jnp.concatenate([high, low], axis=0)
        first = lax.dot_general(wave[parity], both, NT, preferred_element_type=F32)
        second = lax.dot_general(wave_lo[parity], high, NT, preferred_element_type=F32)
        halves.append(((first[:, :128] + first[:, 128:] + second) * SCALE).astype(BF))
    rows = []
    for c in range(2):
        at = slice(c * 512, c * 512 + 512)
        source = jnp.concatenate([halves[0][at], halves[1][at]], axis=0)
        rows.append(jnp.dot(chosen_t[...], source, preferred_element_type=F32).reshape(PARTS, 8, 128))
    out1[...] = jnp.concatenate(rows, axis=1).astype(BF)
    orders = Exchange(me, out1, in1, send_sems.at[1], recv1)
    orders.send_all()
    for load in leg_loads:
        load.wait()
    orders.wait_group(0, PARTS - 1)

    wide[...] = in1[...].astype(F32).reshape(2048, 128)
    blocks = []
    for o in range(8):
        for c in range(2):
            turned = wide[pl.ds(c * 8 + o, 128, stride=16), :].T
            blocks.append(jnp.concatenate([turned[i * F : (i + 1) * F] for i in range(8)], axis=1))
    spectra = jnp.dot(jnp.concatenate(blocks, axis=0).astype(BF), mix[...], preferred_element_type=F32)
    left[...] = (spectra * lat_ref[...]).astype(BF)

    def order(o, carry):
        at = pl.ds(aligned(o * 32, 32), 32)
        coefficients = lax.dot_general(left[at], leg[o], NT, preferred_element_type=F32)
        scaled = (coefficients * love_ref[...]).astype(BF)
        right[at] = jnp.dot(scaled, leg[o], preferred_element_type=F32).astype(BF)
        return carry

    lax.fori_loop(0, 8, order, 0)
    back = jnp.dot(right[...], mix_t[...], preferred_element_type=F32)
    for o in range(8):
        for c in range(2):
            block = back[(o * 2 + c) * F : (o * 2 + c + 1) * F]
            turned = jnp.concatenate([block[:, i * 128 : i * 128 + 128] for i in range(8)], axis=0).T
            wide[pl.ds(c * 8 + o, 128, stride=16), :] = turned
    out2[...] = wide[...].reshape(PACK).astype(BF)
    cycles = Exchange(me, out2, in2, send_sems.at[2], recv2)
    cycles.send_all()
    sums[...] = jnp.zeros_like(sums)
    cell_sums[...] = jnp.zeros_like(cell_sums)
    cycles.wait_group(0, PARTS - 1)

    arrived = in2[...].astype(F32)
    turned = []
    for c in range(2):
        source = arrived[:, c * 8 : c * 8 + 8].reshape(1024, 128).astype(BF)
        placed = jnp.dot(chosen[...], source, preferred_element_type=F32)
        turned.append(
            jnp.concatenate([placed[r * 128 : r * 128 + 128].T for r in range(8)], axis=1).astype(BF)
        )
    sides = []
    for parity in range(2):
        at = slice(parity * 512, parity * 512 + 512)
        source = jnp.concatenate([turned[0][:, at], turned[1][:, at]], axis=1)
        sides.append(
            jnp.dot(source, wave[parity], preferred_element_type=F32)
            + jnp.dot(source, wave_lo[parity], preferred_element_type=F32)
        )
    grid[:, :1024] = (sides[0] + sides[1]) * SCALE
    grid[:, 1024:] = (sides[0] - sides[1]) * SCALE

    def add_slots(b, carry):
        at = pl.ds(aligned(b * 1024, 1024), 1024)
        here = grid[pl.ds(aligned(b // 2 * F, F), F), pl.ds(aligned(b % 2 * 1024, 1024), 1024)]
        values, hots = [], []
        for k in range(3):
            row = sten_ref[k : k + 1, at]
            values.append(spread((here * wts_ref[k : k + 1, at]).astype(BF), row, 64))
            hots.append(lane_one_hot(row))
        sums[...] += lax.dot_general(
            jnp.concatenate(values, axis=1), jnp.concatenate(hots, axis=1), NT,
            preferred_element_type=F32,
        )
        return carry

    lax.fori_loop(0, 16, add_slots, 0)
    for g in range(64):
        out3[2 * g] = sums[g * F : (g + 1) * F, :128].astype(BF)
        out3[2 * g + 1] = sums[g * F : (g + 1) * F, 128:].astype(BF)
    home = Exchange(me, out3, in3, send_sems.at[3], recv3, 8)
    home.send_all()

    def add_cells(b):
        origins = [later(me, PARTS - (b * 8 + r)) for r in range(8)]
        row = jnp.concatenate([send_ref[0, pl.ds(q, 1), :] for q in origins], axis=1)
        values = jnp.concatenate([in3[q] for q in origins], axis=1)
        cell_sums[...] += lax.dot_general(
            spread(values, row, 32), lane_one_hot(row), NT, preferred_element_type=F32
        )

    home.wait_group(0, 7)
    add_cells(0)

    def next_cells(b, carry):
        home.wait_group(b, 8)
        add_cells(b)
        return carry

    lax.fori_loop(1, 16, next_cells, 0)
    for g in range(32):
        loading_ref[:, g * W : (g + 1) * W] = cell_sums[g * F : (g + 1) * F]
    for exchange in (cells, orders, cycles, home):
        exchange.wait_sent()


VM = pl.BlockSpec(memory_space=pltpu.VMEM)
ANY = pl.BlockSpec(memory_space=pl.ANY)


def shape(dims, kind=BF):
    return jax.ShapeDtypeStruct(dims, kind)


def waves():
    m = np.arange(1024)
    n = np.arange(1024)
    angle = 2.0 * math.pi * ((m[:, None] * n[None, :]) % 2048) / 2048.0
    table = np.stack([np.cos(angle), np.sin(angle)])
    table = np.stack([table[:, p::2].reshape(1024, 1024) for p in range(2)])
    high = table.astype(BF)
    return high, (table - high.astype(np.float64)).astype(BF)


def on_device(
    eta, forcing, couplings, neighbors, halo_send, cycle_send, stencil, stencil_weights,
    m_order, lat_weights, love, legendre,
):
    wave, wave_lo = (jnp.asarray(t) for t in waves())
    row = lambda x: x.reshape(1, -1)
    big = (2, 1024, 1024)
    return pl.pallas_call(
        kernel,
        out_shape=(shape(eta.shape, F32), shape(eta.shape, F32)),
        in_specs=[VM] * 6 + [ANY] * 2 + [VM] * 3 + [ANY] * 3,
        out_specs=(VM, VM),
        scratch_shapes=[
            pltpu.VMEM((34 * F, W), BF), pltpu.VMEM((32 * F, W), BF), pltpu.VMEM((F, 2 * W), BF),
            pltpu.VMEM((64 * F, W), BF), pltpu.VMEM((128, 2048), F32), pltpu.VMEM((2048, 128), F32),
            pltpu.VMEM((256, 1024), BF), pltpu.VMEM((256, 1024), BF),
            pltpu.VMEM((64 * F, W), F32), pltpu.VMEM((32 * F, W), F32),
        ]
        + [pltpu.VMEM((1024, 1024), BF)] * 4
        + [
            pltpu.VMEM(stencil.shape, I32), pltpu.VMEM(stencil.shape, F32),
            pltpu.VMEM(legendre.shape, BF), pltpu.VMEM(big, BF), pltpu.VMEM(big, BF),
        ]
        + [pltpu.VMEM(PACK, BF)] * 8
        + [pltpu.SemaphoreType.DMA((n,)) for n in (4, 8, 2, 2, 4, 1, 1, 1, 16)],
        compiler_params=pltpu.CompilerParams(
            collective_id=0, has_side_effects=True, vmem_limit_bytes=60 << 20
        ),
    )(
        eta, forcing, couplings, neighbors, halo_send, cycle_send, stencil, stencil_weights,
        row(m_order), row(lat_weights), row(love), legendre, wave, wave_lo,
    )


def solution(mesh):
    both = ("gx", "gy")
    cells = P(None, both)
    placed = (
        cells, cells, cells, cells, P(both, None), P(both, None, None), cells, cells,
        P(), P(), P(), P(both, None, None),
    )
    return jax.shard_map(
        on_device, mesh=mesh, in_specs=placed, out_specs=(cells, cells), check_vma=False
    )
```

time: 213 us -> 160 us (0.75)
  blocking collectives: 81.2 us -> 0 us
  Pallas kernels: 120 us -> 156 us
  starting transfers between devices: 7.6 us -> 0 us
  local copies, waits for them, and re-layouts: 1.19 us -> 3.74 us
    all_to_all x4 -> x0, blocking collectives: 81.2 us -> none  [exchange(): return lax.all_to_all(blocks, AXES, split_axis=0, concat_axis=0, tiled=True)]
    pallas_call x6 -> x1, Pallas kernels: 120 us -> 156 us  [on_device(): pl.pallas_call(kernel, out_shape=(shape(eta.shape, F32), shape(eta.shape,...]
    ppermute x2 -> x0, starting transfers between devices: 7.6 us -> none  [the longest x1 5.47 us: on_device(): lax.ppermute(low, AXES, [((i + 1) % parts, i) for i in range(parts)])]
    unnamed x4 -> x2, local copies, waits for them, and re-layouts: 1.19 us -> 3.74 us
  transfers between devices with their start and end apart: 2 -> 0, of which waited for: 1 -> 0; matrix products, arithmetic and copies ran while one was open for 0% -> 0% of each run, Pallas kernels for 0% -> 0%
where the time goes in v2:
time: 160 us
  Pallas kernels  156 us (98%)
  local copies, waits for them, and re-layouts  3.74 us (2%)
    pallas_call x1, Pallas kernels, on_device(): pl.pallas_call(kernel, out_shape=(shape(eta.shape, F32), shape(eta.shape,...  156 us
    unnamed x2, local copies, waits for them, and re-layouts  3.74 us

profile of v2, /device:TPU:1, one launch (start us, length us, event | category | flops | bytes accessed | tf_op | source)
XLA Modules:
  0.0 160.2 jit_solution(2916561890193777672)
XLA Ops:
  0.6 155.8 %shard_map.149 = (f32[16,8192]{1,0:T(8,128)}, f32[16,8192]{1,0:T(8,128)}) custom-call(f32[16,8192]{1,0:T(8,128)} %eta_ref.1, f32[16,8192]{1,0:T(8,128)} %forcing_ref.1, f32[3,8192]{1,0:T(4,128)} %coup_ref.1, s32[3,8192]{1,0:T(4,128)} %nbr_ref.1, s32[1,512]{1,0:T(1,128)} %halo_ref.1, s32[1,128,128]{2,1,0:T(8,128)} %send_ref.1, s32[3,16384]{1,0:T(4,128)} %sten_hbm.1, ...), custom_call_target="tpu_custom_call" | custom-call | tf_op jit(solution)/shard_map/pallas_call | solution.py:358
  156.5 1.9 %copy.18 = f32[16,8192]{1,0:T(8,128)} copy(f32[16,8192]{1,0:T(8,128)} %get-tuple-element.4) | data formatting | bytes 1048576
  158.3 1.9 %copy.19 = f32[16,8192]{1,0:T(8,128)} copy(f32[16,8192]{1,0:T(8,128)} %get-tuple-element.5) | data formatting | bytes 1048576

commit v3 on v2

--- a/solution.py
+++ b/solution.py
@@ -75,24 +75,33 @@
         self.tiles(PARTS - 1, 0).wait_send()
 
 
+def as_rows(row):
+    return jnp.broadcast_to(row.astype(F32), (F, row.shape[1])).astype(BF)
+
+
+def marks(lanes, value):
+    n = lanes.shape[1]
+    rows = lax.broadcasted_iota(I32, (W, n), 0).astype(F32).astype(BF)
+    tall = lambda x: jnp.concatenate([x] * (W // F), axis=0)
+    return jnp.where(rows == tall(lanes), tall(value), BF(0))
+
+
 def lane_one_hot(row):
-    n = row.shape[1]
-    return jnp.where(lax.broadcasted_iota(I32, (W, n), 0) == (row & (W - 1)), 1.0, 0.0).astype(BF)
+    return marks(as_rows(row & (W - 1)), jnp.ones((F, row.shape[1]), BF))
 
 
 def gather(table, row):
     n = row.shape[1]
     picked = jnp.dot(table, lane_one_hot(row), preferred_element_type=F32)
     group = jnp.broadcast_to(row >> 8, (F, n))
-    out = picked[:F]
-    for g in range(1, table.shape[0] // F):
+    out = jnp.zeros((F, n), F32)
+    for g in range(table.shape[0] // F):
         out = jnp.where(group == g, picked[g * F : (g + 1) * F], out)
     return out
 
 
 def spread(values, row, groups):
-    n = row.shape[1]
-    group = jnp.broadcast_to((row >> 8).astype(F32), (F, n)).astype(BF)
+    group = as_rows(row >> 8)
     return jnp.concatenate(
         [jnp.where(group == BF(g), values, BF(0)) for g in range(groups)], axis=0
     )
@@ -110,7 +119,7 @@
     eta_ref, forcing_ref, coup_ref, nbr_ref, halo_ref, send_ref, sten_hbm, wts_hbm, m_ref, lat_ref,
     love_ref, leg_hbm, wave_hbm, wave_lo_hbm,
     stepped_ref, loading_ref,
-    table, table2, rim, slots, grid, wide, left, right, sums, cell_sums, chosen, chosen_t, mix, mix_t,
+    table, table2, rim, slots, grid, wide, left, right, sums, cell_sums, halo, turn, turn_t,
     sten_ref, wts_ref, leg, wave, wave_lo,
     out0, in0, out1, in1, out2, in2, out3, in3,
     load_sems, leg_sems, halo_send, halo_recv, send_sems, recv0, recv1, recv2, recv3,
@@ -130,24 +139,33 @@
         )
     ]
     leg_loads = [pltpu.make_async_copy(leg_hbm.at[o], leg.at[o], leg_sems.at[o]) for o in range(8)]
-    for load in loads + leg_loads:
+    for load in loads:
         load.start()
 
     for g in range(32):
         table[g * F : (g + 1) * F] = eta_ref[:, g * W : (g + 1) * W].astype(BF)
-    rim[...] = gather(table[: 32 * F], halo_ref[...]).astype(BF)
-    slot = order_slot(m_ref[...])
-    for r in range(8):
-        at = slice(r * 128, r * 128 + 128)
-        row = lax.broadcasted_iota(I32, (128, 1024), 0) + r * 128
-        lane = lax.broadcasted_iota(I32, (128, 1024), 1)
-        chosen[at] = jnp.where(slot == row, 1.0, 0.0).astype(BF)
-        column = jnp.broadcast_to(slot[:, at].astype(F32), (128, 128)).T.astype(I32)
-        for s in range(8):
-            side = slice(s * 128, s * 128 + 128)
-            chosen_t[at, side] = jnp.where(column == lane[:, side], 1.0, 0.0).astype(BF)
-        mix[at] = jnp.where((lane >> 3) + (lane & 7) * 128 == row, 1.0, 0.0).astype(BF)
-        mix_t[at] = jnp.where((row >> 3) + (row & 7) * 128 == lane, 1.0, 0.0).astype(BF)
+    rim[...] = gather(table[...], halo_ref[...]).astype(BF)
+
+    def step(b, carry):
+        at = pl.ds(aligned(b * 1024, 1024), 1024)
+        here = eta_ref[:, at]
+        total = here + forcing_ref[:, at]
+        sides = [None, None]
+        for k in range(3):
+            row = nbr_ref[k : k + 1, at]
+            weight = coup_ref[k : k + 1, at]
+            total += weight * (gather(table[...], row) - here)
+            weights = jnp.broadcast_to(weight, (F, 1024)).astype(BF)
+            for i in range(2):
+                lanes = jnp.where(row >> 8 == 32 + i, row & (W - 1), -1)
+                part = marks(as_rows(lanes), weights)
+                sides[i] = part if k == 0 else sides[i] + part
+        stepped_ref[:, at] = total
+        for i in range(2):
+            leg[b // 2, pl.ds(aligned(b % 2 * 512 + i * W, W), W)] = sides[i]
+        return carry
+
+    lax.fori_loop(0, 8, step, 0)
 
     pl.semaphore_wait(barrier, PARTS - 1)
     halos = []
@@ -155,45 +173,49 @@
         halos.append(
             pltpu.make_async_remote_copy(
                 src_ref=rim.at[:, pl.ds(start, W)],
-                dst_ref=table.at[pl.ds((32 + i) * F, F)],
+                dst_ref=halo.at[:, pl.ds(i * W, W)],
                 send_sem=halo_send.at[i],
                 recv_sem=halo_recv.at[i],
                 device_id=place(to),
                 device_id_type=MESH,
             )
         )
-    for halo in halos:
-        halo.start()
-    for halo in halos:
-        halo.wait()
-
-    def step(b, carry):
-        at = pl.ds(aligned(b * 512, 512), 512)
-        here = eta_ref[:, at]
-        total = here + forcing_ref[:, at]
-        for k in range(3):
-            total += coup_ref[k : k + 1, at] * (gather(table[...], nbr_ref[k : k + 1, at]) - here)
+    for copy in halos:
+        copy.start()
+    slot = order_slot(m_ref[...])
+    lane = lax.broadcasted_iota(I32, (128, 1024), 1)
+    for r in range(8):
+        at = slice(r * 128, r * 128 + 128)
+        column = jnp.broadcast_to(slot[:, at].astype(F32), (128, 128)).T.astype(I32)
+        for s in range(8):
+            side = slice(s * 128, s * 128 + 128)
+            turn[at, side] = jnp.where(column == lane[:, side], 1.0, 0.0).astype(BF)
+    for copy in halos:
+        copy.wait()
+    for b in range(8):
+        at = slice(b * 1024, b * 1024 + 1024)
+        around = leg[b // 2, b % 2 * 512 : b % 2 * 512 + 512]
+        total = stepped_ref[:, at] + jnp.dot(halo[...], around, preferred_element_type=F32)
         stepped_ref[:, at] = total
         rounded = total.astype(BF)
-        table2[pl.ds(aligned(b * 32, 32), F)] = rounded[:, :W]
-        table2[pl.ds(aligned(b * 32 + F, F), F)] = rounded[:, W:]
-        return carry
-
-    lax.fori_loop(0, 16, step, 0)
+        for i in range(4):
+            g = b * 4 + i
+            table2[g * F : (g + 1) * F] = rounded[:, i * W : (i + 1) * W]
+    for load in leg_loads:
+        load.start()
 
     cells = Exchange(me, out0, in0, send_sems.at[0], recv0)
 
     def send(b, carry):
-        for half in range(2):
-            steps = [b * 8 + half * 4 + r for r in range(4)]
-            row = jnp.concatenate([send_ref[0, pl.ds(later(me, s), 1), :] for s in steps], axis=1)
-            got = gather(table2[...], row).astype(BF)
-            for r in range(4):
-                out0[later(me, steps[r])] = got[:, r * 128 : r * 128 + 128]
-                if half + r == 0:
-                    pl.when(b > 0)(functools.partial(cells.send, steps[r]))
-                else:
-                    cells.send(steps[r])
+        steps = [b * 8 + r for r in range(8)]
+        row = jnp.concatenate([send_ref[0, pl.ds(later(me, s), 1), :] for s in steps], axis=1)
+        got = gather(table2[...], row).astype(BF)
+        for r in range(8):
+            out0[later(me, steps[r])] = got[:, r * 128 : r * 128 + 128]
+            if r == 0:
+                pl.when(b > 0)(functools.partial(cells.send, steps[r]))
+            else:
+                cells.send(steps[r])
         return carry
 
     lax.fori_loop(0, 16, send, 0)
@@ -206,14 +228,14 @@
         slots[g * F : (g + 1) * F, 128:] = in0[2 * g + 1]
 
     def pick(b, carry):
-        at = pl.ds(aligned(b * 512, 512), 512)
-        total = jnp.zeros((F, 512), F32)
+        at = pl.ds(aligned(b * 1024, 1024), 1024)
+        total = jnp.zeros((F, 1024), F32)
         for k in range(3):
             total += gather(slots[...], sten_ref[k : k + 1, at]) * wts_ref[k : k + 1, at]
-        grid[pl.ds(aligned(b // 4 * F, F), F), pl.ds(aligned(b % 4 * 512, 512), 512)] = total
-        return carry
-
-    lax.fori_loop(0, 32, pick, 0)
+        grid[pl.ds(aligned(b // 2 * F, F), F), pl.ds(aligned(b % 2 * 1024, 1024), 1024)] = total
+        return carry
+
+    lax.fori_loop(0, 16, pick, 0, unroll=2)
 
     halves = []
     for parity in range(2):
@@ -229,10 +251,15 @@
     for c in range(2):
         at = slice(c * 512, c * 512 + 512)
         source = jnp.concatenate([halves[0][at], halves[1][at]], axis=0)
-        rows.append(jnp.dot(chosen_t[...], source, preferred_element_type=F32).reshape(PARTS, 8, 128))
+        rows.append(jnp.dot(turn[...], source, preferred_element_type=F32).reshape(PARTS, 8, 128))
     out1[...] = jnp.concatenate(rows, axis=1).astype(BF)
     orders = Exchange(me, out1, in1, send_sems.at[1], recv1)
     orders.send_all()
+    for r in range(8):
+        at = slice(r * 128, r * 128 + 128)
+        row = lax.broadcasted_iota(I32, (128, 1024), 0) + r * 128
+        turn[at] = jnp.where((lane >> 3) + (lane & 7) * 128 == row, 1.0, 0.0).astype(BF)
+        turn_t[at] = jnp.where((row >> 3) + (row & 7) * 128 == lane, 1.0, 0.0).astype(BF)
     for load in leg_loads:
         load.wait()
     orders.wait_group(0, PARTS - 1)
@@ -243,7 +270,7 @@
         for c in range(2):
             turned = wide[pl.ds(c * 8 + o, 128, stride=16), :].T
             blocks.append(jnp.concatenate([turned[i * F : (i + 1) * F] for i in range(8)], axis=1))
-    spectra = jnp.dot(jnp.concatenate(blocks, axis=0).astype(BF), mix[...], preferred_element_type=F32)
+    spectra = jnp.dot(jnp.concatenate(blocks, axis=0).astype(BF), turn[...], preferred_element_type=F32)
     left[...] = (spectra * lat_ref[...]).astype(BF)
 
     def order(o, carry):
@@ -253,8 +280,8 @@
         right[at] = jnp.dot(scaled, leg[o], preferred_element_type=F32).astype(BF)
         return carry
 
-    lax.fori_loop(0, 8, order, 0)
-    back = jnp.dot(right[...], mix_t[...], preferred_element_type=F32)
+    lax.fori_loop(0, 8, order, 0, unroll=4)
+    back = jnp.dot(right[...], turn_t[...], preferred_element_type=F32)
     for o in range(8):
         for c in range(2):
             block = back[(o * 2 + c) * F : (o * 2 + c + 1) * F]
@@ -263,6 +290,9 @@
     out2[...] = wide[...].reshape(PACK).astype(BF)
     cycles = Exchange(me, out2, in2, send_sems.at[2], recv2)
     cycles.send_all()
+    for r in range(8):
+        row = lax.broadcasted_iota(I32, (128, 1024), 0) + r * 128
+        turn[r * 128 : r * 128 + 128] = jnp.where(slot == row, 1.0, 0.0).astype(BF)
     sums[...] = jnp.zeros_like(sums)
     cell_sums[...] = jnp.zeros_like(cell_sums)
     cycles.wait_group(0, PARTS - 1)
@@ -271,7 +301,7 @@
     turned = []
     for c in range(2):
         source = arrived[:, c * 8 : c * 8 + 8].reshape(1024, 128).astype(BF)
-        placed = jnp.dot(chosen[...], source, preferred_element_type=F32)
+        placed = jnp.dot(turn[...], source, preferred_element_type=F32)
         turned.append(
             jnp.concatenate([placed[r * 128 : r * 128 + 128].T for r in range(8)], axis=1).astype(BF)
         )
@@ -287,8 +317,8 @@
     grid[:, 1024:] = (sides[0] - sides[1]) * SCALE
 
     def add_slots(b, carry):
-        at = pl.ds(aligned(b * 1024, 1024), 1024)
-        here = grid[pl.ds(aligned(b // 2 * F, F), F), pl.ds(aligned(b % 2 * 1024, 1024), 1024)]
+        at = pl.ds(aligned(b * 2048, 2048), 2048)
+        here = grid[pl.ds(aligned(b * F, F), F), :]
         values, hots = [], []
         for k in range(3):
             row = sten_ref[k : k + 1, at]
@@ -300,7 +330,7 @@
         )
         return carry
 
-    lax.fori_loop(0, 16, add_slots, 0)
+    lax.fori_loop(0, 8, add_slots, 0)
     for g in range(64):
         out3[2 * g] = sums[g * F : (g + 1) * F, :128].astype(BF)
         out3[2 * g + 1] = sums[g * F : (g + 1) * F, 128:].astype(BF)
@@ -361,12 +391,12 @@
         in_specs=[VM] * 6 + [ANY] * 2 + [VM] * 3 + [ANY] * 3,
         out_specs=(VM, VM),
         scratch_shapes=[
-            pltpu.VMEM((34 * F, W), BF), pltpu.VMEM((32 * F, W), BF), pltpu.VMEM((F, 2 * W), BF),
+            pltpu.VMEM((32 * F, W), BF), pltpu.VMEM((32 * F, W), BF), pltpu.VMEM((F, 2 * W), BF),
             pltpu.VMEM((64 * F, W), BF), pltpu.VMEM((128, 2048), F32), pltpu.VMEM((2048, 128), F32),
             pltpu.VMEM((256, 1024), BF), pltpu.VMEM((256, 1024), BF),
             pltpu.VMEM((64 * F, W), F32), pltpu.VMEM((32 * F, W), F32),
         ]
-        + [pltpu.VMEM((1024, 1024), BF)] * 4
+        + [pltpu.VMEM((F, 2 * W), BF), pltpu.VMEM((1024, 1024), BF), pltpu.VMEM((1024, 1024), BF)]
         + [
             pltpu.VMEM(stencil.shape, I32), pltpu.VMEM(stencil.shape, F32),
             pltpu.VMEM(legendre.shape, BF), pltpu.VMEM(big, BF), pltpu.VMEM(big, BF),
@@ -380,8 +410,6 @@
         eta, forcing, couplings, neighbors, halo_send, cycle_send, stencil, stencil_weights,
         row(m_order), row(lat_weights), row(love), legendre, wave, wave_lo,
     )
-
-
 def solution(mesh):
     both = ("gx", "gy")
     cells = P(None, both)

time: 160 us -> 151 us (0.944)
  Pallas kernels: 156 us -> 146 us
    pallas_call x1, Pallas kernels: 156 us -> 146 us  [on_device(): pl.pallas_call(kernel, out_shape=(shape(eta.shape, F32), shape(eta.shape,...]
where the time goes in v3:
time: 151 us
  Pallas kernels  146 us (97%)
  local copies, waits for them, and re-layouts  3.74 us (2%)
    pallas_call x1, Pallas kernels, on_device(): pl.pallas_call(kernel, out_shape=(shape(eta.shape, F32), shape(eta.shape,...  146 us
    unnamed x2, local copies, waits for them, and re-layouts  3.74 us

profile of v3, /device:TPU:1, one launch (start us, length us, event | category | flops | bytes accessed | tf_op | source)
XLA Modules:
  0.0 150.7 jit_solution(16249379317047162977)
XLA Ops:
  0.6 146.3 %shard_map.149 = (f32[16,8192]{1,0:T(8,128)}, f32[16,8192]{1,0:T(8,128)}) custom-call(f32[16,8192]{1,0:T(8,128)} %eta_ref.1, f32[16,8192]{1,0:T(8,128)} %forcing_ref.1, f32[3,8192]{1,0:T(4,128)} %coup_ref.1, s32[3,8192]{1,0:T(4,128)} %nbr_ref.1, s32[1,512]{1,0:T(1,128)} %halo_ref.1, s32[1,128,128]{2,1,0:T(8,128)} %send_ref.1, s32[3,16384]{1,0:T(4,128)} %sten_hbm.1, ...), custom_call_target="tpu_custom_call" | custom-call | tf_op jit(solution)/shard_map/pallas_call | solution.py:388
  146.9 1.9 %copy.18 = f32[16,8192]{1,0:T(8,128)} copy(f32[16,8192]{1,0:T(8,128)} %get-tuple-element.4) | data formatting | bytes 1048576
  148.8 1.9 %copy.19 = f32[16,8192]{1,0:T(8,128)} copy(f32[16,8192]{1,0:T(8,128)} %get-tuple-element.5) | data formatting | bytes 1048576

commit v4 on v3

--- a/solution.py
+++ b/solution.py
@@ -49,12 +49,15 @@
     def keep(self):
         self.into[self.me] = self.out[self.me]
 
-    def send_all(self):
+    def send_range(self, first, end):
         def one(steps, carry):
             self.send(steps)
             return carry
 
-        lax.fori_loop(1, PARTS, one, 0)
+        lax.fori_loop(first, end, one, 0)
+
+    def send_all(self):
+        self.send_range(1, PARTS)
         self.keep()
 
     def tiles(self, count, sem):
@@ -204,7 +207,7 @@
     for load in leg_loads:
         load.start()
 
-    cells = Exchange(me, out0, in0, send_sems.at[0], recv0)
+    cells = Exchange(me, out0, in0, send_sems.at[0], recv0, PARTS // 2)
 
     def send(b, carry):
         steps = [b * 8 + r for r in range(8)]
@@ -222,20 +225,26 @@
     cells.keep()
     for load in loads:
         load.wait()
-    cells.wait_group(0, PARTS - 1)
-    for g in range(64):
-        slots[g * F : (g + 1) * F, :128] = in0[2 * g]
-        slots[g * F : (g + 1) * F, 128:] = in0[2 * g + 1]
-
-    def pick(b, carry):
-        at = pl.ds(aligned(b * 1024, 1024), 1024)
-        total = jnp.zeros((F, 1024), F32)
-        for k in range(3):
-            total += gather(slots[...], sten_ref[k : k + 1, at]) * wts_ref[k : k + 1, at]
-        grid[pl.ds(aligned(b // 2 * F, F), F), pl.ds(aligned(b % 2 * 1024, 1024), 1024)] = total
-        return carry
-
-    lax.fori_loop(0, 16, pick, 0, unroll=2)
+
+    for half in range(2):
+        cells.wait_group(half, 63 + half)
+        for g in range(32 * half, 32 * half + 32):
+            slots[g * F : (g + 1) * F, :128] = in0[later(me, PARTS - 2 * g)]
+            slots[g * F : (g + 1) * F, 128:] = in0[later(me, PARTS - 2 * g - 1)]
+
+        def pick(b, carry):
+            at = pl.ds(aligned(b * 2048, 2048), 2048)
+            into = pl.ds(aligned(b * F, F), F)
+            total = jnp.zeros((F, 2048), F32) if half == 0 else grid[into, :]
+            for k in range(3):
+                row = sten_ref[k : k + 1, at]
+                below = (me - (row >> 7) + PARTS) & (PARTS - 1)
+                row = (below << 7) + (row & 127) - half * 8192
+                total += gather(slots[half * 512 : half * 512 + 512], row) * wts_ref[k : k + 1, at]
+            grid[into, :] = total
+            return carry
+
+        lax.fori_loop(0, 8, pick, 0)
 
     halves = []
     for parity in range(2):
@@ -316,26 +325,32 @@
     grid[:, :1024] = (sides[0] + sides[1]) * SCALE
     grid[:, 1024:] = (sides[0] - sides[1]) * SCALE
 
-    def add_slots(b, carry):
-        at = pl.ds(aligned(b * 2048, 2048), 2048)
-        here = grid[pl.ds(aligned(b * F, F), F), :]
-        values, hots = [], []
-        for k in range(3):
-            row = sten_ref[k : k + 1, at]
-            values.append(spread((here * wts_ref[k : k + 1, at]).astype(BF), row, 64))
-            hots.append(lane_one_hot(row))
-        sums[...] += lax.dot_general(
-            jnp.concatenate(values, axis=1), jnp.concatenate(hots, axis=1), NT,
-            preferred_element_type=F32,
-        )
-        return carry
-
-    lax.fori_loop(0, 8, add_slots, 0)
-    for g in range(64):
-        out3[2 * g] = sums[g * F : (g + 1) * F, :128].astype(BF)
-        out3[2 * g + 1] = sums[g * F : (g + 1) * F, 128:].astype(BF)
     home = Exchange(me, out3, in3, send_sems.at[3], recv3, 8)
-    home.send_all()
+    for half in range(2):
+        rows = slice(half * 512, half * 512 + 512)
+
+        def add_slots(b, carry):
+            at = pl.ds(aligned(b * 2048, 2048), 2048)
+            here = grid[pl.ds(aligned(b * F, F), F), :]
+            values, hots = [], []
+            for k in range(3):
+                row = sten_ref[k : k + 1, at]
+                above = ((row >> 7) - me + PARTS) & (PARTS - 1)
+                row = (above << 7) + (row & 127) - half * 8192
+                values.append(spread((here * wts_ref[k : k + 1, at]).astype(BF), row, 32))
+                hots.append(lane_one_hot(row))
+            sums[rows] += lax.dot_general(
+                jnp.concatenate(values, axis=1), jnp.concatenate(hots, axis=1), NT,
+                preferred_element_type=F32,
+            )
+            return carry
+
+        lax.fori_loop(0, 8, add_slots, 0)
+        for g in range(32 * half, 32 * half + 32):
+            out3[later(me, 2 * g)] = sums[g * F : (g + 1) * F, :128].astype(BF)
+            out3[later(me, 2 * g + 1)] = sums[g * F : (g + 1) * F, 128:].astype(BF)
+        home.send_range(max(half * 64, 1), half * 64 + 64)
+    home.keep()
 
     def add_cells(b):
         origins = [later(me, PARTS - (b * 8 + r)) for r in range(8)]
@@ -402,7 +417,7 @@
             pltpu.VMEM(legendre.shape, BF), pltpu.VMEM(big, BF), pltpu.VMEM(big, BF),
         ]
         + [pltpu.VMEM(PACK, BF)] * 8
-        + [pltpu.SemaphoreType.DMA((n,)) for n in (4, 8, 2, 2, 4, 1, 1, 1, 16)],
+        + [pltpu.SemaphoreType.DMA((n,)) for n in (4, 8, 2, 2, 4, 2, 1, 1, 16)],
         compiler_params=pltpu.CompilerParams(
             collective_id=0, has_side_effects=True, vmem_limit_bytes=60 << 20
         ),

time: 151 us -> 147 us (0.974)
  Pallas kernels: 146 us -> 142 us
    pallas_call x1, Pallas kernels: 146 us -> 142 us  [on_device(): pl.pallas_call(kernel, out_shape=(shape(eta.shape, F32), shape(eta.shape,...]
where the time goes in v4:
time: 147 us
  Pallas kernels  142 us (97%)
  local copies, waits for them, and re-layouts  3.74 us (3%)
    pallas_call x1, Pallas kernels, on_device(): pl.pallas_call(kernel, out_shape=(shape(eta.shape, F32), shape(eta.shape,...  142 us
    unnamed x2, local copies, waits for them, and re-layouts  3.74 us

profile of v4, /device:TPU:1, one launch (start us, length us, event | category | flops | bytes accessed | tf_op | source)
XLA Modules:
  0.0 146.8 jit_solution(12863880062529325460)
XLA Ops:
  0.6 142.5 %shard_map.149 = (f32[16,8192]{1,0:T(8,128)}, f32[16,8192]{1,0:T(8,128)}) custom-call(f32[16,8192]{1,0:T(8,128)} %eta_ref.1, f32[16,8192]{1,0:T(8,128)} %forcing_ref.1, f32[3,8192]{1,0:T(4,128)} %coup_ref.1, s32[3,8192]{1,0:T(4,128)} %nbr_ref.1, s32[1,512]{1,0:T(1,128)} %halo_ref.1, s32[1,128,128]{2,1,0:T(8,128)} %send_ref.1, s32[3,16384]{1,0:T(4,128)} %sten_hbm.1, ...), custom_call_target="tpu_custom_call" | custom-call | tf_op jit(solution)/shard_map/pallas_call | solution.py:403
  143.1 1.9 %copy.18 = f32[16,8192]{1,0:T(8,128)} copy(f32[16,8192]{1,0:T(8,128)} %get-tuple-element.4) | data formatting | bytes 1048576
  145.0 1.9 %copy.19 = f32[16,8192]{1,0:T(8,128)} copy(f32[16,8192]{1,0:T(8,128)} %get-tuple-element.5) | data formatting | bytes 1048576
